TPU v7x, 32 devices: a whole 2x2x4 slice. The times are simulated.
32 devices in a mesh: row: 4 (over y, core), col: 8 (over z, x).
Axes of the slice: x: 2, y: 2, z: 4, core: 2. Of those that a mesh axis runs over, the one named last changes fastest.
Arguments:
- features: bfloat16 [4096, 128], P(('row', 'col')), may hold values from -6 to 6
- norm_weight: float32 [4096], P(('row', 'col')), may hold values from 0.01767767 to 0.110485435
- weight_in: bfloat16 [128, 256], replicated, may hold values from -6 to 6
- weight_out: bfloat16 [256, 128], replicated, may hold values from -6 to 6
- labels: int32 [4096], P(('row', 'col')), may hold values from 0 to 127
- tile_slot: int32 [32, 128], P(('row', 'col')), may hold values from 0 to 31
- tile_edges: int32 [32, 128, 2, 512], P(('row', 'col')), may hold values from 0 to 127
- tile_count: int32 [32], P(('row', 'col')), may hold values from 32 to 128, as said below
Outputs:
- grad_in: float32 [128, 256], replicated
- grad_out: float32 [256, 128], replicated
- loss: float32 [], replicated
Inputs may be any that keep to these rules, and one draw needn't show every extreme that they name: `tile_slot`: position p of a slot covers the tile whose target rows start at 128 * (p // 4) and whose source columns start at 128 * (p % 4) within the device's block; a position may occur in several slots. Entry k of a slot marks row tile_edges[s, 0, k] and column tile_edges[s, 1, k] of its slot's tile; repeated entries count again. `tile_count`: slots at and after this number are not live; in every draw some device has all 128 slots live and another device only 32.
All inputs are finite; a program needn't handle non-finite values.
Results may differ from a plain program's by a relative error of at most 0.0084.
Values may be sent and summed in bfloat16 or wider, within the bound.
A program may use at most 64 MiB of HBM per device.

v0:
```python
import jax
import jax.numpy as jnp
from jax import lax
from jax.sharding import PartitionSpec as P

TILE = 128


SOFTCAP = 15.0
LOSS_SCALE = 1024.0
HIGHEST = lax.Precision.HIGHEST
CONTRACT_ROWS = (((0,), (0,)), ((), ()))


def densify(tile_slot, tile_edges, tile_count, row_group, col_group):
    tile_side = TILE
    col_tiles = col_group // tile_side
    row_tiles = row_group // tile_side
    slot_total = tile_slot.shape[0]
    offsets = jnp.arange(tile_side, dtype=jnp.int32)
    row_onehot = (tile_edges[:, 0, :, None] == offsets[None, None, :]).astype(jnp.bfloat16)
    col_onehot = (tile_edges[:, 1, :, None] == offsets[None, None, :]).astype(jnp.bfloat16)
    slot_tiles = jnp.einsum(
        "ser,sec->src", row_onehot, col_onehot, preferred_element_type=jnp.float32
    )
    slot_tiles = slot_tiles.astype(jnp.bfloat16).reshape(slot_total, tile_side * tile_side)
    slot_live = jnp.arange(slot_total, dtype=jnp.int32) < tile_count
    places = jnp.arange(row_tiles * col_tiles, dtype=jnp.int32)
    place_onehot = ((tile_slot[:, None] == places[None, :]) & slot_live[:, None]).astype(
        jnp.bfloat16
    )
    placed = lax.dot_general(
        place_onehot, slot_tiles, CONTRACT_ROWS, preferred_element_type=jnp.float32
    )
    placed = placed.astype(jnp.bfloat16).reshape(row_tiles, col_tiles, tile_side, tile_side)
    return placed.transpose(0, 2, 1, 3).reshape(row_group, col_group)


def gather_targets(values):
    return lax.all_gather(values, "col", axis=0, tiled=True)


def sum_sources(partial_sums):
    return lax.psum_scatter(partial_sums, "row", scatter_dimension=0, tiled=True)


def per_device(
    features, norm_weight, weight_in, weight_out, labels, tile_slot, tile_edges, tile_count
):
    row_size = lax.axis_size("row")
    col_size = lax.axis_size("col")
    node_rows = features.shape[0]
    total_nodes = node_rows * row_size * col_size
    adjacency = densify(
        tile_slot[0], tile_edges[0], tile_count[0], node_rows * col_size, node_rows * row_size
    )
    node_scale = norm_weight[:, None]
    normed = (node_scale * features.astype(jnp.float32)).astype(jnp.bfloat16)
    source_one = jnp.dot(normed, weight_in, preferred_element_type=jnp.float32)
    gathered_one = lax.all_gather(source_one, "row", axis=0, tiled=True)
    forward_one = jnp.dot(adjacency.astype(jnp.float32), gathered_one, precision=HIGHEST)
    projected = lax.psum_scatter(forward_one, "col", scatter_dimension=0, tiled=True)
    pre_hidden = node_scale * (projected + source_one)
    hidden = jax.nn.relu(pre_hidden).astype(jnp.bfloat16)
    source_two = (
        node_scale * jnp.dot(hidden, weight_out, preferred_element_type=jnp.float32)
    ).astype(jnp.bfloat16)
    gathered_two = lax.all_gather(source_two, "row", axis=0, tiled=True)
    forward_two = jnp.dot(adjacency, gathered_two, preferred_element_type=jnp.float32)
    logits = node_scale * (
        lax.psum_scatter(forward_two, "col", scatter_dimension=0, tiled=True)
        + source_two.astype(jnp.float32)
    )
    capped = SOFTCAP * jnp.tanh(logits / SOFTCAP)
    exp_capped = jnp.exp(capped)
    exp_total = jnp.sum(exp_capped, axis=1, keepdims=True)
    one_hot = (labels[:, None] == jnp.arange(capped.shape[1], dtype=jnp.int32)[None, :]).astype(
        jnp.float32
    )
    loss_local = jnp.sum(jnp.log(exp_total[:, 0]) - jnp.sum(capped * one_hot, axis=1))
    d_logits = (
        LOSS_SCALE
        / total_nodes
        * (exp_capped / exp_total - one_hot)
        * (1.0 - (capped / SOFTCAP) ** 2)
    )
    back_two = (node_scale * d_logits).astype(jnp.bfloat16)
    backward_two = lax.dot_general(
        adjacency, gather_targets(back_two), CONTRACT_ROWS, preferred_element_type=jnp.float32
    )
    d_source_two = node_scale * (sum_sources(backward_two) + back_two.astype(jnp.float32))
    grad_out_local = lax.dot_general(
        hidden.astype(jnp.float32), d_source_two, CONTRACT_ROWS, precision=HIGHEST
    )
    d_hidden = lax.dot_general(
        d_source_two, weight_out.astype(jnp.float32), (((1,), (1,)), ((), ())), precision=HIGHEST
    )
    back_one = (node_scale * jnp.where(pre_hidden > 0, d_hidden, 0.0)).astype(jnp.bfloat16)
    gathered_back = gather_targets(back_one)
    backward_one = lax.dot_general(
        adjacency, gathered_back, CONTRACT_ROWS, preferred_element_type=jnp.float32
    )
    d_source_one = sum_sources(backward_one) + back_one.astype(jnp.float32)
    grad_in_local = lax.dot_general(
        normed.astype(jnp.float32), d_source_one, CONTRACT_ROWS, precision=HIGHEST
    )
    grad_in, grad_out, loss_sum = lax.psum(
        (grad_in_local, grad_out_local, loss_local), ("row", "col")
    )
    return (grad_in, grad_out, loss_sum / total_nodes)


def solution(mesh):
    in_specs = (
        P(("row", "col"), None),
        P(("row", "col")),
        P(),
        P(),
        P(("row", "col")),
        P(("row", "col"), None),
        P(("row", "col"), None, None, None),
        P(("row", "col")),
    )
    out_specs = (P(), P(), P())
    return jax.shard_map(
        per_device, mesh=mesh, in_specs=in_specs, out_specs=out_specs, check_vma=False
    )
```

profile of v0, /device:TPU:0, one launch (start us, length us, event | category | flops | bytes accessed | tf_op | source)
XLA Modules:
  0.0 426.0 jit_solution(7901533714446784060)
XLA Ops:
  7.2 0.0 copy-start
  7.2 0.0 reduce-scatter.5.cloned.1.call-start
  7.2 1.7 fusion.37
  9.0 7.9 %iota_compare_fusion.17 = pred[128,512,128]{1,2,0:T(32,128)(4,1)} fusion(s32[128,512]{1,0:T(8,128)S(1)} %get-tuple-element.10), kind=kLoop, calls=%fused_computation.1.clone.clone.clone.clone.2 | loop fusion | flops 8388608 | bytes 8650752 | tf_op jit(solution)/shard_map/ser,sec->src/dot_general | solution.py:23
  17.6 0.0 copy-start.6
  17.6 14.4 %fusion.5 = bf16[128,128,128]{2,1,0:T(8,128)(2,1)S(1)} fusion(s32[128,512]{1,0:T(8,128)S(1)} %get-tuple-element.9, pred[128,512,128]{1,2,0:T(32,128)(4,1)} %iota_compare_fusion.17), kind=kOutput, calls=%fused_computation.8 | convolution fusion | flops 2157969408 | bytes 12845056 | tf_op jit(solution)/shard_map/ser,sec->src/dot_general | solution.py:23
  32.0 0.0 copy-start.4
  32.0 0.0 copy-start.2
  32.0 0.0 copy-start.3
  32.1 0.0 copy-done.6
  32.1 0.0 copy-start.5
  32.1 2.6 fusion.6
  34.7 0.2 copy.23
  34.9 0.7 copy.15
  35.7 0.0 copy-done.4
  35.7 0.1 copy.14
  35.8 0.0 copy-done.2
  35.8 0.0 copy-done.3
  35.8 0.2 fusion.34
  36.0 8.6 %all_gather.12 = f32[512,256]{1,0:T(8,128)S(1)} all-gather(f32[128,256]{1,0:T(8,128)S(1)} %fusion.34), channel_id=1, replica_groups=mesh['row'=4,'col'=8] {'row'}, dimensions={0}, use_global_device_ids=true | all-gather | bytes 655360 | tf_op jit(solution)/shard_map/all_gather | solution.py:60
  44.6 2.2 fusion.18
  46.8 0.0 reduce-scatter.5.cloned.1.call-update
  46.9 0.0 reduce-scatter.7.cloned.1.call-start
  46.9 64.4 %reduce-scatter.5.cloned.1.call-done = f32[128,256]{1,0:T(8,128)} async-done(((f32[1024,256]{1,0:T(8,128)}), f32[128,256]{1,0:T(8,128)}) %reduce-scatter.5.cloned.1.call-update) | async-done | bytes 131088 | tf_op jit(solution)/shard_map/reduce_scatter | solution.py:62
  111.3 0.0 copy-done
  111.3 0.0 copy-start.1
  111.3 1.2 fusion.11
  112.6 5.4 %all_gather.13 = bf16[512,128]{0,1:T(8,128)(2,1)S(1)} all-gather(bf16[128,128]{0,1:T(8,128)(2,1)S(1)} %fusion.11), channel_id=1, replica_groups=mesh['row'=4,'col'=8] {'row'}, dimensions={0}, use_global_device_ids=true | all-gather | bytes 163840 | tf_op jit(solution)/shard_map/all_gather | solution.py:68
  118.0 1.1 fusion.16
  119.1 0.0 reduce-scatter.7.cloned.1.call-update
  119.1 0.0 reduce-scatter.9.cloned.1.call-start
  119.2 61.5 %reduce-scatter.7.cloned.1.call-done = f32[128,128]{0,1:T(8,128)} async-done(((f32[1024,128]{0,1:T(8,128)}), f32[128,128]{0,1:T(8,128)}) %reduce-scatter.7.cloned.1.call-update) | async-done | bytes 65552 | tf_op jit(solution)/shard_map/reduce_scatter | solution.py:71
  180.7 0.0 copy-done.5
  180.7 0.9 select_reduce_fusion
  181.6 0.9 multiply_convert_fusion
  182.5 26.7 %all_gather.14 = bf16[1024,128]{0,1:T(8,128)(2,1)S(1)} all-gather(bf16[128,128]{0,1:T(8,128)(2,1)S(1)} %multiply_convert_fusion), channel_id=1, replica_groups=mesh['row'=4,'col'=8] {'col'}, dimensions={0}, use_global_device_ids=true | all-gather | bytes 294912 | tf_op jit(solution)/shard_map/all_gather | solution.py:40
  209.2 1.2 fusion.14
  210.3 0.0 reduce-scatter.9.cloned.1.call-update
  210.4 0.0 reduce-scatter.11.cloned.1.call-start
  210.4 17.7 %reduce-scatter.9.cloned.1.call-done = f32[128,128]{0,1:T(8,128)} async-done(((f32[512,128]{0,1:T(8,128)}), f32[128,128]{0,1:T(8,128)}) %reduce-scatter.9.cloned.1.call-update) | async-done | bytes 65552 | tf_op jit(solution)/shard_map/reduce_scatter | solution.py:44
  228.1 1.2 fusion.10
  229.3 31.4 %all_gather.15 = bf16[1024,256]{1,0:T(8,128)(2,1)S(1)} all-gather(bf16[128,256]{1,0:T(8,128)(2,1)S(1)} %fusion.10), channel_id=1, replica_groups=mesh['row'=4,'col'=8] {'col'}, dimensions={0}, use_global_device_ids=true | all-gather | bytes 589824 | tf_op jit(solution)/shard_map/all_gather | solution.py:40
  260.7 1.2 fusion.12
  262.0 0.0 reduce-scatter.11.cloned.1.call-update
  262.0 0.0 all-reduce.3.cloned.1.call-start
  262.0 0.0 copy-done.1
  262.0 1.8 fusion.29
  263.9 20.0 %reduce-scatter.11.cloned.1.call-done = f32[128,256]{1,0:T(8,128)} async-done(((f32[512,256]{1,0:T(8,128)}), f32[128,256]{1,0:T(8,128)}) %reduce-scatter.11.cloned.1.call-update) | async-done | bytes 131088 | tf_op jit(solution)/shard_map/reduce_scatter | solution.py:44
  283.9 1.8 fusion.24
  285.6 0.0 all-reduce.3.cloned.1.call-update
  285.7 0.6 subtract_reduce_fusion
  286.3 39.5 %psum.23 = f32[]{:T(128)} all-reduce(f32[]{:T(128)} %subtract_reduce_fusion), channel_id=1, replica_groups=mesh['row'=4,'col'=8] {'row','col'}, use_global_device_ids=true, to_apply=%region_9.10 | all-reduce | flops 1 | bytes 8 | tf_op jit(solution)/shard_map/psum | solution.py:107
  326.5 88.7 %all-reduce.3.cloned.1.call-done = (f32[128,256]{1,0:T(8,128)}, f32[256,128]{1,0:T(8,128)}) async-done(((f32[128,256]{1,0:T(8,128)}, f32[256,128]{1,0:T(8,128)}), (f32[128,256]{1,0:T(8,128)}, f32[256,128]{1,0:T(8,128)})) %all-reduce.3.cloned.1.call-update) | async-done | bytes 262160 | tf_op jit(solution)/shard_map/psum | solution.py:107
  415.2 1.6 copy.54
  416.7 1.6 copy.55
  (2 shorter events, 0.0 us)
Async XLA Ops:
  7.2 104.2 %copy-start = (bf16[256,128]{1,0:T(8,128)(2,1)S(1)}, bf16[256,128]{1,0:T(8,128)(2,1)}, u32[]{:S(2)}) copy-start(bf16[256,128]{1,0:T(8,128)(2,1)} %param.11) | copy-start | bytes 196612
  7.2 104.1 %reduce-scatter.5.cloned.1.call-start = ((), (), s32[]{:S(2)}) async-start(), calls=%async_computation.4 | async-start | bytes 1179648 | tf_op jit(solution)/shard_map/reduce_scatter | solution.py:62
  17.6 14.5 %copy-start.6 = (s32[1,128]{1,0:T(1,128)S(1)}, s32[1,128]{1,0:T(1,128)}, u32[]{:S(2)}) copy-start(s32[1,128]{1,0:T(1,128)} %param.13) | copy-start | bytes 1540
  32.0 3.6 copy-start.4
  32.0 3.7 copy-start.2
  32.0 3.7 copy-start.3
  32.1 148.6 %copy-start.5 = (s32[128]{0:T(128)S(1)}, s32[128]{0:T(128)}, u32[]{:S(2)}) copy-start(s32[128]{0:T(128)} %param.12) | copy-start | bytes 1540
  46.9 133.8 %reduce-scatter.7.cloned.1.call-start = ((), (), s32[]{:S(2)}) async-start(), calls=%async_computation.5 | async-start | bytes 589824 | tf_op jit(solution)/shard_map/reduce_scatter | solution.py:71
  111.3 150.7 %copy-start.1 = (f32[128,256]{1,0:T(8,128)S(1)}, f32[128,256]{1,0:T(8,128)}, u32[]{:S(2)}) copy-start(f32[128,256]{1,0:T(8,128)} %reduce-scatter.5.cloned.1.call-done) | copy-start | bytes 393220
  119.1 109.0 %reduce-scatter.9.cloned.1.call-start = ((), (), s32[]{:S(2)}) async-start(), calls=%async_computation.6 | async-start | bytes 327680 | tf_op jit(solution)/shard_map/reduce_scatter | solution.py:44
  210.4 73.5 %reduce-scatter.11.cloned.1.call-start = ((), (), s32[]{:S(2)}) async-start(), calls=%async_computation.7 | async-start | bytes 655360 | tf_op jit(solution)/shard_map/reduce_scatter | solution.py:44
  262.0 153.2 %all-reduce.3.cloned.1.call-start = ((), (), s32[]{:S(2)}) async-start(), calls=%async_computation.8 | async-start | bytes 524288 | tf_op jit(solution)/shard_map/psum | solution.py:107
Sparse Core Ops, SparseCore 0:
  47.0 64.3 reduce-scatter.4
  119.2 61.3 reduce-scatter.6
  210.5 17.5 reduce-scatter.8
  262.1 21.7 reduce-scatter.10
  290.0 125.1 all-reduce.2
where the time goes:
time: 426 us
  waiting for transfers between devices  252 us (59%)
  blocking collectives  112 us (26%)
  matrix products  29 us (7%)
  between operations  16.4 us (4%)
  other arithmetic  10.3 us (2%)
  local copies, waits for them, and re-layouts  6.02 us (1%)
    psum x1, waiting for transfers between devices, per_device(): lax.psum((grad_in_local, grad_out_local, loss_local), ('row', 'col'))  88.7 us
    reduce_scatter x1, waiting for transfers between devices, per_device(): lax.psum_scatter(forward_one, 'col', scatter_dimension=0, tiled=True)  64.4 us
    reduce_scatter x1, waiting for transfers between devices, per_device(): lax.psum_scatter(forward_two, 'col', scatter_dimension=0, tiled=True)  61.5 us
    all_gather x2, blocking collectives, gather_targets(): return lax.all_gather(values, 'col', axis=0, tiled=True)  58.1 us
    psum x1, blocking collectives, per_device(): lax.psum((grad_in_local, grad_out_local, loss_local), ('row', 'col'))  39.5 us
    reduce_scatter x2, waiting for transfers between devices, sum_sources(): lax.psum_scatter(partial_sums, 'row', scatter_dimension=0, tiled=True)  37.7 us
    dot_general x1, matrix products, densify(): jnp.einsum('ser,sec->src', row_onehot, col_onehot, preferred_element_type...  14.4 us
    all_gather x1, blocking collectives, per_device(): gathered_one = lax.all_gather(source_one, 'row', axis=0, tiled=True)  8.65 us
  transfers between devices with their start and end apart: 5, of which 5 were waited for; matrix products, arithmetic and copies ran while one was open for 1% of the time, Pallas kernels for 0%

commit v1 on v0

v1 whole, which is shorter than its diff:
```python
import functools

import jax
import jax.numpy as jnp
from jax import lax
from jax.experimental import pallas as pl
from jax.experimental.pallas import tpu as pltpu
from jax.sharding import PartitionSpec as P

TILE = 128
SOFTCAP = 15.0
LOSS_SCALE = 1024.0
UNROLL = 4
LOSS_ROWS = 16
MESH = pl.DeviceIdType.MESH
F32 = jnp.float32
BF16 = jnp.bfloat16
VMEM_LIMIT = 56 * 1024 * 1024


def dot(a, b, ca=1, cb=0):
    return lax.dot_general(a, b, (((ca,), (cb,)), ((), ())), preferred_element_type=F32)


def split2(x):
    hi = x.astype(BF16)
    return hi, (x - hi.astype(F32)).astype(BF16)


def densify_kernel(row_tiles, col_tiles, count_ref, slot_ref, edges_ref, out_ref, acc):
    places = row_tiles * col_tiles
    count = count_ref[0]
    acc[...] = jnp.zeros_like(acc)
    entries = edges_ref.shape[3]
    iota = lax.broadcasted_iota(jnp.int32, (TILE, entries), 0)

    def body(step, carry):
        found = []
        for u in range(UNROLL):
            s = step * UNROLL + u
            edges = edges_ref[0, s]
            rows = (iota == edges[0:1, :]).astype(F32).astype(BF16)
            cols = (iota == edges[1:2, :]).astype(F32).astype(BF16)
            found.append((jnp.where(s < count, slot_ref[0, s], places), dot(rows, cols, 1, 1)))
        for p, tile in found:
            acc[p] += tile
        return carry

    lax.fori_loop(0, (count + UNROLL - 1) // UNROLL, body, 0)
    for r in range(row_tiles):
        for c in range(col_tiles):
            out_ref[r * TILE : (r + 1) * TILE, c * TILE : (c + 1) * TILE] = acc[
                r * col_tiles + c
            ].astype(BF16)


def densify(tile_slot, tile_edges, tile_count, row_group, col_group):
    row_tiles, col_tiles = row_group // TILE, col_group // TILE
    return pl.pallas_call(
        functools.partial(densify_kernel, row_tiles, col_tiles),
        out_shape=jax.ShapeDtypeStruct((row_group, col_group), BF16),
        in_specs=[
            pl.BlockSpec(memory_space=pltpu.SMEM),
            pl.BlockSpec(memory_space=pltpu.SMEM),
            pl.BlockSpec(memory_space=pltpu.VMEM),
        ],
        out_specs=pl.BlockSpec(memory_space=pltpu.VMEM),
        scratch_shapes=[pltpu.VMEM((row_tiles * col_tiles + 1, TILE, TILE), F32)],
        compiler_params=pltpu.CompilerParams(vmem_limit_bytes=VMEM_LIMIT),
        name="densify",
    )(tile_count, tile_slot, tile_edges)


def step_kernel(
    R, C, nd, adj, feat, norm, w_in, w_out, labels,
    grad_in, grad_out, loss_out,
    gath_one, part_one, recv_one, gath_two, part_two, recv_two,
    gath_back, part_back, recv_back, part_grad, recv_grad, slots_grad, full_grad,
    send_sem, recv_sem,
):
    i = lax.axis_index("row")
    j = lax.axis_index("col")
    total_nodes = nd * R * C
    chunk = full_grad.shape[0] // C
    pending = []

    def row_peer(k):
        return (lax.rem(i + k, R), j)

    def col_peer(k):
        return (i, lax.rem(j + k, C))

    def send(phase, k, peer, src, dst):
        copy = pltpu.make_async_remote_copy(
            src_ref=src, dst_ref=dst,
            send_sem=send_sem.at[phase, k - 1], recv_sem=recv_sem.at[phase, k - 1],
            device_id=peer, device_id_type=MESH,
        )
        copy.start()
        pending.append(copy)
        return copy

    def arrive(copies):
        for copy in copies:
            copy.wait_recv()

    barrier = pltpu.get_barrier_semaphore()
    for k in range(1, R):
        pl.semaphore_signal(barrier, inc=1, device_id=row_peer(k), device_id_type=MESH)
    for k in range(1, C):
        pl.semaphore_signal(barrier, inc=1, device_id=col_peer(k), device_id_type=MESH)

    scale = jnp.transpose(jnp.broadcast_to(norm[...], (nd, nd)))
    normed = (scale * feat[...].astype(F32)).astype(BF16)
    mine = pl.ds(pl.multiple_of(i * nd, nd), nd)
    gath_one[mine, :] = normed
    pl.semaphore_wait(barrier, R + C - 2)

    def block_of(t):
        return adj[pl.ds(pl.multiple_of(t * nd, nd), nd), :]

    arrive([send(0, k, row_peer(k), gath_one.at[mine], gath_one.at[mine]) for k in range(1, R)])
    values = gath_one[...]
    copies = []
    for k in range(1, C):
        part_one[k - 1] = dot(block_of(lax.rem(j + k, C)), values)
        copies.append(send(1, k, col_peer(k), part_one.at[k - 1], recv_one.at[k - 1]))
    mixed = dot(block_of(j), values) + normed.astype(F32)
    for k in range(1, C):
        copies[k - 1].wait_recv()
        mixed = mixed + recv_one[k - 1]
    m_hi, m_lo = split2(mixed)
    m_least = (mixed - m_hi.astype(F32) - m_lo.astype(F32)).astype(BF16)
    w = w_in[...]
    pre_hidden = jnp.concatenate([scale, scale], axis=1) * (
        dot(m_hi, w) + (dot(m_lo, w) + dot(m_least, w))
    )
    hidden = jnp.maximum(pre_hidden, 0.0).astype(BF16)
    source_two = (scale * dot(hidden, w_out[...])).astype(BF16)
    gath_two[mine, :] = source_two
    arrive([send(2, k, row_peer(k), gath_two.at[mine], gath_two.at[mine]) for k in range(1, R)])
    values = gath_two[...]
    copies = []
    for k in range(1, C):
        part_two[k - 1] = dot(block_of(lax.rem(j + k, C)), values).astype(BF16)
        copies.append(send(3, k, col_peer(k), part_two.at[k - 1], recv_two.at[k - 1]))
    logits = dot(block_of(j), values) + source_two.astype(F32)
    for k in range(1, C):
        copies[k - 1].wait_recv()
        logits = logits + recv_two[k - 1].astype(F32)
    logits = scale * logits
    ratio = jnp.tanh(logits * (1.0 / SOFTCAP))
    capped = SOFTCAP * ratio
    exp_capped = jnp.exp(capped)
    exp_total = jnp.sum(exp_capped, axis=1, keepdims=True)
    label_rows = jnp.transpose(jnp.broadcast_to(labels[...].astype(F32), (nd, nd)))
    one_hot = jnp.where(
        label_rows == lax.broadcasted_iota(jnp.int32, (nd, nd), 1).astype(F32), 1.0, 0.0
    )
    node_loss = jnp.log(exp_total) - jnp.sum(capped * one_hot, axis=1, keepdims=True)
    loss_local = jnp.sum(node_loss, axis=0, keepdims=True)
    d_logits = (LOSS_SCALE / total_nodes) * (exp_capped / exp_total - one_hot) * (
        1.0 - ratio * ratio
    )
    back_two = (scale * d_logits).astype(BF16)

    upper = lax.broadcasted_iota(jnp.int32, (LOSS_ROWS, TILE), 0) < LOSS_ROWS // 2

    def loss_rows(value):
        value = jnp.broadcast_to(value, (LOSS_ROWS, TILE))
        hi, lo = split2(value)
        return jnp.where(upper, hi.astype(F32), lo.astype(F32)).astype(BF16)

    def read_loss(rows):
        rows = rows.astype(F32)
        return rows[0:1, :] + rows[LOSS_ROWS // 2 : LOSS_ROWS // 2 + 1, :]

    gath_back[j, :nd, :] = back_two
    gath_back[j, nd:, :] = loss_rows(loss_local)
    arrive([send(4, k, col_peer(k), gath_back.at[j], gath_back.at[j]) for k in range(1, C)])
    loss_col = read_loss(gath_back[0, nd:, :])
    for k in range(1, C):
        loss_col = loss_col + read_loss(gath_back[k, nd:, :])
    values_t = jnp.transpose(
        jnp.concatenate([gath_back[k, :nd, :] for k in range(C)], axis=0).astype(F32)
    ).astype(BF16)
    rows_loss = loss_rows(loss_col)

    def back_of(t):
        return dot(values_t, adj[:, pl.ds(pl.multiple_of(t * nd, nd), nd)])

    copies = []
    for k in range(1, R):
        part_back[k - 1, :nd, :] = back_of(lax.rem(i + k, R)).astype(BF16)
        part_back[k - 1, nd:, :] = rows_loss
        copies.append(send(5, k, row_peer(k), part_back.at[k - 1], recv_back.at[i]))
    recv_back[i, nd:, :] = rows_loss
    summed = back_of(i)
    arrive(copies)
    recv_back[i, :nd, :] = jnp.zeros((nd, nd), BF16)
    loss_all = read_loss(recv_back[0, nd:, :])
    for k in range(1, R):
        loss_all = loss_all + read_loss(recv_back[k, nd:, :])
    for k in range(R):
        summed = summed + recv_back[k, :nd, :].astype(F32)
    loss_out[...] = jnp.broadcast_to(loss_all * (1.0 / total_nodes), loss_out.shape)
    d_source = scale * (jnp.transpose(summed) + back_two.astype(F32))
    d_hi, d_lo = split2(d_source)
    d_hidden = dot(d_hi, w_out[...], 1, 1) + dot(d_lo, w_out[...], 1, 1)
    back_one = jnp.where(
        pre_hidden > 0, jnp.concatenate([scale, scale], axis=1) * d_hidden, 0.0
    ).astype(BF16)
    local_out = dot(hidden, d_hi, 0, 0) + dot(hidden, d_lo, 0, 0)
    local_in = dot(m_hi, back_one, 0, 0) + dot(m_lo, back_one, 0, 0)

    fan_in, half = local_in.shape[0], TILE
    hid = local_in.shape[1]
    for h in range(hid // half):
        part_grad[h * fan_in : (h + 1) * fan_in, :] = local_in[:, h * half : (h + 1) * half].astype(
            BF16
        )
    base = fan_in * (hid // half)
    part_grad[base:, :] = local_out.astype(BF16)

    def rows_of(t):
        return pl.ds(pl.multiple_of(t * chunk, chunk), chunk)

    copies = [
        send(6, k, col_peer(k), part_grad.at[rows_of(lax.rem(j + k, C))], recv_grad.at[k - 1])
        for k in range(1, C)
    ]
    total = part_grad[rows_of(j), :].astype(F32)
    for k in range(1, C):
        copies[k - 1].wait_recv()
        total = total + recv_grad[k - 1].astype(F32)
    slots_grad[i] = total.astype(BF16)
    arrive([send(7, k, row_peer(k), slots_grad.at[i], slots_grad.at[i]) for k in range(1, R)])
    total = slots_grad[0].astype(F32)
    for k in range(1, R):
        total = total + slots_grad[k].astype(F32)
    full_grad[rows_of(j), :] = total.astype(BF16)
    arrive(
        [
            send(8, k, col_peer(k), full_grad.at[rows_of(j)], full_grad.at[rows_of(j)])
            for k in range(1, C)
        ]
    )
    for h in range(hid // half):
        grad_in[:, h * half : (h + 1) * half] = full_grad[h * fan_in : (h + 1) * fan_in, :].astype(
            F32
        )
    grad_out[...] = full_grad[base:, :].astype(F32)
    for copy in pending:
        copy.wait_send()


def per_device(
    features, norm_weight, weight_in, weight_out, labels, tile_slot, tile_edges, tile_count
):
    R = lax.axis_size("row")
    C = lax.axis_size("col")
    nd, fan_in = features.shape
    hid, classes = weight_out.shape
    adjacency = densify(tile_slot, tile_edges, tile_count, nd * C, nd * R)
    grad_rows = (fan_in * hid + hid * classes) // TILE
    chunk = grad_rows // C
    most = max(R, C) - 1
    vmem = pl.BlockSpec(memory_space=pltpu.VMEM)
    grad_in, grad_out, loss = pl.pallas_call(
        functools.partial(step_kernel, R, C, nd),
        out_shape=(
            jax.ShapeDtypeStruct((fan_in, hid), F32),
            jax.ShapeDtypeStruct((hid, classes), F32),
            jax.ShapeDtypeStruct((1, TILE), F32),
        ),
        in_specs=[vmem] * 6,
        out_specs=(vmem, vmem, vmem),
        scratch_shapes=[
            pltpu.VMEM((R * nd, fan_in), BF16),
            pltpu.VMEM((C - 1, nd, fan_in), F32),
            pltpu.VMEM((C - 1, nd, fan_in), F32),
            pltpu.VMEM((R * nd, classes), BF16),
            pltpu.VMEM((C - 1, nd, classes), BF16),
            pltpu.VMEM((C - 1, nd, classes), BF16),
            pltpu.VMEM((C, nd + LOSS_ROWS, classes), BF16),
            pltpu.VMEM((R - 1, nd + LOSS_ROWS, classes), BF16),
            pltpu.VMEM((R, nd + LOSS_ROWS, classes), BF16),
            pltpu.VMEM((grad_rows, TILE), BF16),
            pltpu.VMEM((C - 1, chunk, TILE), BF16),
            pltpu.VMEM((R, chunk, TILE), BF16),
            pltpu.VMEM((grad_rows, TILE), BF16),
            pltpu.SemaphoreType.DMA((9, most)),
            pltpu.SemaphoreType.DMA((9, most)),
        ],
        compiler_params=pltpu.CompilerParams(
            collective_id=0, has_side_effects=True, vmem_limit_bytes=VMEM_LIMIT
        ),
        name="train_step",
    )(adjacency, features, norm_weight[None, :], weight_in, weight_out, labels[None, :])
    return grad_in, grad_out, loss[0, 0]


def solution(mesh):
    in_specs = (
        P(("row", "col"), None),
        P(("row", "col")),
        P(),
        P(),
        P(("row", "col")),
        P(("row", "col"), None),
        P(("row", "col"), None, None, None),
        P(("row", "col")),
    )
    out_specs = (P(), P(), P())
    return jax.shard_map(
        per_device, mesh=mesh, in_specs=in_specs, out_specs=out_specs, check_vma=False
    )
```

time: 426 us -> 76.8 us (0.18)
  waiting for transfers between devices: 252 us -> 0 us
  blocking collectives: 112 us -> 0 us
  Pallas kernels: 0 us -> 72.1 us
  matrix products: 29 us -> 0 us
  between operations: 16.4 us -> 2.46 us
  other arithmetic: 10.3 us -> 0 us
    reduce_scatter x4 -> x0, waiting for transfers between devices: 164 us -> none  [the longest x1 64.4 us: per_device(): lax.psum_scatter(forward_one, 'col', scatter_dimension=0, tiled=True)]
    psum x1 -> x0, waiting for transfers between devices: 88.7 us -> none  [per_device(): lax.psum((grad_in_local, grad_out_local, loss_local), ('row', 'col'))]
    all_gather x4 -> x0, blocking collectives: 72.2 us -> none  [the longest x2 58.1 us: gather_targets(): return lax.all_gather(values, 'col', axis=0, tiled=True)]
    pallas_call x0 -> x2, Pallas kernels: none -> 72.1 us  [the longest x1 60.2 us: per_device(): pl.pallas_call(functools.partial(step_kernel, R, C, nd), out_shape=(jax.S...]
    psum x1 -> x0, blocking collectives: 39.5 us -> none  [per_device(): lax.psum((grad_in_local, grad_out_local, loss_local), ('row', 'col'))]
    dot_general x11 -> x0, matrix products: 29 us -> none  [the longest x1 14.4 us: densify(): jnp.einsum('ser,sec->src', row_onehot, col_onehot, preferred_element_type...]
    dot_general x1 -> x0, other arithmetic: 7.88 us -> none  [densify(): jnp.einsum('ser,sec->src', row_onehot, col_onehot, preferred_element_type...]
  transfers between devices with their start and end apart: 5 -> 0, of which waited for: 5 -> 0; matrix products, arithmetic and copies ran while one was open for 1% -> 0% of each run, Pallas kernels for 0% -> 0%
where the time goes in v1:
time: 76.8 us
  Pallas kernels  72.1 us (94%)
  between operations  2.46 us (3%)
  local copies, waits for them, and re-layouts  2.27 us (3%)
    pallas_call x1, Pallas kernels, per_device(): pl.pallas_call(functools.partial(step_kernel, R, C, nd), out_shape=(jax.S...  60.2 us
    pallas_call x1, Pallas kernels, densify(): pl.pallas_call(functools.partial(densify_kernel, row_tiles, col_tiles), o...  11.9 us
    unnamed x6, local copies, waits for them, and re-layouts  2.27 us

profile of v1, /device:TPU:0, one launch (start us, length us, event | category | flops | bytes accessed | tf_op | source)
XLA Modules:
  0.0 76.8 jit_solution(6788090887514920120)
XLA Ops:
  1.3 11.9 %densify.1.adj = bf16[1024,512]{1,0:T(8,128)(2,1)} custom-call(s32[1]{0:T(128)S(6)} %copy.14.count_ref, s32[1,128]{1,0:T(1,128)} %slot_ref.1, s32[1,128,2,512]{3,2,1,0:T(2,128)} %edges_ref.1), custom_call_target="tpu_custom_call" | custom-call | tf_op jit(solution)/shard_map/densify/pallas_call | solution.py:59
  13.2 60.2 %train_step.1 = (f32[128,256]{1,0:T(8,128)}, f32[256,128]{1,0:T(8,128)}, f32[1,128]{1,0:T(1,128)}) custom-call(bf16[1024,512]{1,0:T(8,128)(2,1)} %densify.1.adj, bf16[128,128]{1,0:T(8,128)(2,1)} %feat.1, f32[1,128]{1,0:T(1,128)} %bitcast.4, bf16[128,256]{1,0:T(8,128)(2,1)} %w_in.1, bf16[256,128]{1,0:T(8,128)(2,1)} %w_out.1, s32[1,128]{1,0:T(1,128)} %bitcast.5), custom_call_target="tpu_custom_call" | custom-call | tf_op jit(solution)/shard_map/train_step/pallas_call | solution.py:269
  73.4 0.0 copy-start
  73.4 1.6 %copy.15 = f32[128,256]{1,0:T(8,128)} copy(f32[128,256]{1,0:T(8,128)} %get-tuple-element.12) | data formatting | bytes 262144
  75.0 0.0 copy-done
  75.0 0.0 copy-start.1
  75.0 0.7 copy.16
  75.7 0.0 copy-done.1
Async XLA Ops:
  73.4 1.6 %copy-start = (f32[256,128]{1,0:T(8,128)S(1)}, f32[256,128]{1,0:T(8,128)}, u32[]{:S(2)}) copy-start(f32[256,128]{1,0:T(8,128)} %get-tuple-element.13) | copy-start | bytes 393220
  75.0 0.7 copy-start.1

commit v2 on v1

--- a/solution.py
+++ b/solution.py
@@ -10,7 +10,7 @@
 TILE = 128
 SOFTCAP = 15.0
 LOSS_SCALE = 1024.0
-UNROLL = 4
+UNROLL = 16
 LOSS_ROWS = 16
 MESH = pl.DeviceIdType.MESH
 F32 = jnp.float32
@@ -74,7 +74,7 @@
 def step_kernel(
     R, C, nd, adj, feat, norm, w_in, w_out, labels,
     grad_in, grad_out, loss_out,
-    gath_one, part_one, recv_one, gath_two, part_two, recv_two,
+    gath_one, part_one, recv_one, part_low, recv_low, gath_two, part_two, recv_two,
     gath_back, part_back, recv_back, part_grad, recv_grad, slots_grad, full_grad,
     send_sem, recv_sem,
 ):
@@ -123,20 +123,20 @@
     values = gath_one[...]
     copies = []
     for k in range(1, C):
-        part_one[k - 1] = dot(block_of(lax.rem(j + k, C)), values)
+        part_one[k - 1], part_low[k - 1] = split2(dot(block_of(lax.rem(j + k, C)), values))
         copies.append(send(1, k, col_peer(k), part_one.at[k - 1], recv_one.at[k - 1]))
+    low_copies = [
+        send(9, k, col_peer(k), part_low.at[k - 1], recv_low.at[k - 1]) for k in range(1, C)
+    ]
     mixed = dot(block_of(j), values) + normed.astype(F32)
     for k in range(1, C):
         copies[k - 1].wait_recv()
-        mixed = mixed + recv_one[k - 1]
+        mixed = mixed + recv_one[k - 1].astype(F32)
+    w = w_in[...]
+    scale_wide = jnp.concatenate([scale, scale], axis=1)
     m_hi, m_lo = split2(mixed)
-    m_least = (mixed - m_hi.astype(F32) - m_lo.astype(F32)).astype(BF16)
-    w = w_in[...]
-    pre_hidden = jnp.concatenate([scale, scale], axis=1) * (
-        dot(m_hi, w) + (dot(m_lo, w) + dot(m_least, w))
-    )
-    hidden = jnp.maximum(pre_hidden, 0.0).astype(BF16)
-    source_two = (scale * dot(hidden, w_out[...])).astype(BF16)
+    hidden_ahead = jnp.maximum(scale_wide * (dot(m_hi, w) + dot(m_lo, w)), 0.0).astype(BF16)
+    source_two = (scale * dot(hidden_ahead, w_out[...])).astype(BF16)
     gath_two[mine, :] = source_two
     arrive([send(2, k, row_peer(k), gath_two.at[mine], gath_two.at[mine]) for k in range(1, R)])
     values = gath_two[...]
@@ -177,7 +177,17 @@
 
     gath_back[j, :nd, :] = back_two
     gath_back[j, nd:, :] = loss_rows(loss_local)
-    arrive([send(4, k, col_peer(k), gath_back.at[j], gath_back.at[j]) for k in range(1, C)])
+    copies = [send(4, k, col_peer(k), gath_back.at[j], gath_back.at[j]) for k in range(1, C)]
+    arrive(low_copies)
+    low = recv_low[0].astype(F32)
+    for k in range(2, C):
+        low = low + recv_low[k - 1].astype(F32)
+    mixed = mixed + low
+    m_hi, m_lo = split2(mixed)
+    m_least = (mixed - m_hi.astype(F32) - m_lo.astype(F32)).astype(BF16)
+    pre_hidden = scale_wide * (dot(m_hi, w) + (dot(m_lo, w) + dot(m_least, w)))
+    hidden = jnp.maximum(pre_hidden, 0.0).astype(BF16)
+    arrive(copies)
     loss_col = read_loss(gath_back[0, nd:, :])
     for k in range(1, C):
         loss_col = loss_col + read_loss(gath_back[k, nd:, :])
@@ -208,7 +218,7 @@
     d_hi, d_lo = split2(d_source)
     d_hidden = dot(d_hi, w_out[...], 1, 1) + dot(d_lo, w_out[...], 1, 1)
     back_one = jnp.where(
-        pre_hidden > 0, jnp.concatenate([scale, scale], axis=1) * d_hidden, 0.0
+        pre_hidden > 0, scale_wide * d_hidden, 0.0
     ).astype(BF16)
     local_out = dot(hidden, d_hi, 0, 0) + dot(hidden, d_lo, 0, 0)
     local_in = dot(m_hi, back_one, 0, 0) + dot(m_lo, back_one, 0, 0)
@@ -277,8 +287,10 @@
         out_specs=(vmem, vmem, vmem),
         scratch_shapes=[
             pltpu.VMEM((R * nd, fan_in), BF16),
-            pltpu.VMEM((C - 1, nd, fan_in), F32),
-            pltpu.VMEM((C - 1, nd, fan_in), F32),
+            pltpu.VMEM((C - 1, nd, fan_in), BF16),
+            pltpu.VMEM((C - 1, nd, fan_in), BF16),
+            pltpu.VMEM((C - 1, nd, fan_in), BF16),
+            pltpu.VMEM((C - 1, nd, fan_in), BF16),
             pltpu.VMEM((R * nd, classes), BF16),
             pltpu.VMEM((C - 1, nd, classes), BF16),
             pltpu.VMEM((C - 1, nd, classes), BF16),
@@ -289,8 +301,8 @@
             pltpu.VMEM((C - 1, chunk, TILE), BF16),
             pltpu.VMEM((R, chunk, TILE), BF16),
             pltpu.VMEM((grad_rows, TILE), BF16),
-            pltpu.SemaphoreType.DMA((9, most)),
-            pltpu.SemaphoreType.DMA((9, most)),
+            pltpu.SemaphoreType.DMA((10, most)),
+            pltpu.SemaphoreType.DMA((10, most)),
         ],
         compiler_params=pltpu.CompilerParams(
             collective_id=0, has_side_effects=True, vmem_limit_bytes=VMEM_LIMIT

time: 76.8 us -> 71 us (0.924)
  Pallas kernels: 72.1 us -> 66.5 us
    pallas_call x1, Pallas kernels: 11.9 us -> 7.98 us  [densify(): pl.pallas_call(functools.partial(densify_kernel, row_tiles, col_tiles), o...]
    pallas_call x1, Pallas kernels: 60.2 us -> 58.5 us  [per_device(): pl.pallas_call(functools.partial(step_kernel, R, C, nd), out_shape=(jax.S...]
where the time goes in v2:
time: 71 us; the launch traced here: 71.3 us
  Pallas kernels  66.5 us (94%)
  between operations  2.46 us (3%)
  local copies, waits for them, and re-layouts  2.27 us (3%)
    pallas_call x1, Pallas kernels, per_device(): pl.pallas_call(functools.partial(step_kernel, R, C, nd), out_shape=(jax.S...  58.5 us
    pallas_call x1, Pallas kernels, densify(): pl.pallas_call(functools.partial(densify_kernel, row_tiles, col_tiles), o...  7.98 us
    unnamed x6, local copies, waits for them, and re-layouts  2.27 us

profile of v2, /device:TPU:0, one launch (start us, length us, event | category | flops | bytes accessed | tf_op | source)
XLA Modules:
  0.0 71.3 jit_solution(8522956417441421811)
XLA Ops:
  1.3 8.0 %densify.1.adj = bf16[1024,512]{1,0:T(8,128)(2,1)} custom-call(s32[1]{0:T(128)S(6)} %copy.14.count_ref, s32[1,128]{1,0:T(1,128)} %slot_ref.1, s32[1,128,2,512]{3,2,1,0:T(2,128)} %edges_ref.1), custom_call_target="tpu_custom_call" | custom-call | tf_op jit(solution)/shard_map/densify/pallas_call | solution.py:59
  9.3 58.5 %train_step.1 = (f32[128,256]{1,0:T(8,128)}, f32[256,128]{1,0:T(8,128)}, f32[1,128]{1,0:T(1,128)}) custom-call(bf16[1024,512]{1,0:T(8,128)(2,1)} %densify.1.adj, bf16[128,128]{1,0:T(8,128)(2,1)} %feat.1, f32[1,128]{1,0:T(1,128)} %bitcast.4, bf16[128,256]{1,0:T(8,128)(2,1)} %w_in.1, bf16[256,128]{1,0:T(8,128)(2,1)} %w_out.1, s32[1,128]{1,0:T(1,128)} %bitcast.5), custom_call_target="tpu_custom_call" | custom-call | tf_op jit(solution)/shard_map/train_step/pallas_call | solution.py:279
  67.8 0.0 copy-start
  67.8 1.6 %copy.15 = f32[128,256]{1,0:T(8,128)} copy(f32[128,256]{1,0:T(8,128)} %get-tuple-element.12) | data formatting | bytes 262144
  69.4 0.0 copy-done
  69.4 0.0 copy-start.1
  69.4 0.7 copy.16
  70.1 0.0 copy-done.1
Async XLA Ops:
  67.8 1.6 %copy-start = (f32[256,128]{1,0:T(8,128)S(1)}, f32[256,128]{1,0:T(8,128)}, u32[]{:S(2)}) copy-start(f32[256,128]{1,0:T(8,128)} %get-tuple-element.13) | copy-start | bytes 393220
  69.4 0.7 copy-start.1

commit v3 on v2

--- a/solution.py
+++ b/solution.py
@@ -10,7 +10,7 @@
 TILE = 128
 SOFTCAP = 15.0
 LOSS_SCALE = 1024.0
-UNROLL = 16
+UNROLL = 32
 LOSS_ROWS = 16
 MESH = pl.DeviceIdType.MESH
 F32 = jnp.float32
@@ -32,15 +32,16 @@
     count = count_ref[0]
     acc[...] = jnp.zeros_like(acc)
     entries = edges_ref.shape[3]
-    iota = lax.broadcasted_iota(jnp.int32, (TILE, entries), 0)
+    iota = lax.broadcasted_iota(jnp.int32, (TILE, entries), 0).astype(F32).astype(BF16)
+    ones, zeros = jnp.ones(iota.shape, BF16), jnp.zeros(iota.shape, BF16)
 
     def body(step, carry):
         found = []
         for u in range(UNROLL):
             s = step * UNROLL + u
-            edges = edges_ref[0, s]
-            rows = (iota == edges[0:1, :]).astype(F32).astype(BF16)
-            cols = (iota == edges[1:2, :]).astype(F32).astype(BF16)
+            edges = edges_ref[0, s].astype(F32).astype(BF16)
+            rows = jnp.where(iota == edges[0:1, :], ones, zeros)
+            cols = jnp.where(iota == edges[1:2, :], ones, zeros)
             found.append((jnp.where(s < count, slot_ref[0, s], places), dot(rows, cols, 1, 1)))
         for p, tile in found:
             acc[p] += tile

time: 71 us -> 70 us (0.986)
  Pallas kernels: 66.5 us -> 64.9 us
    pallas_call x1, Pallas kernels: 7.98 us -> 6.12 us  [densify(): pl.pallas_call(functools.partial(densify_kernel, row_tiles, col_tiles), o...]
where the time goes in v3:
time: 70 us; the launch traced here: 69.6 us
  Pallas kernels  64.9 us (93%)
  between operations  2.46 us (4%)
  local copies, waits for them, and re-layouts  2.27 us (3%)
    pallas_call x1, Pallas kernels, per_device(): pl.pallas_call(functools.partial(step_kernel, R, C, nd), out_shape=(jax.S...  58.8 us
    pallas_call x1, Pallas kernels, densify(): pl.pallas_call(functools.partial(densify_kernel, row_tiles, col_tiles), o...  6.12 us
    unnamed x6, local copies, waits for them, and re-layouts  2.27 us

profile of v3, /device:TPU:0, one launch (start us, length us, event | category | flops | bytes accessed | tf_op | source)
XLA Modules:
  0.0 69.6 jit_solution(11266353483848924085)
XLA Ops:
  1.3 6.1 %densify.1.adj = bf16[1024,512]{1,0:T(8,128)(2,1)} custom-call(s32[1]{0:T(128)S(6)} %copy.14.count_ref, s32[1,128]{1,0:T(1,128)} %slot_ref.1, s32[1,128,2,512]{3,2,1,0:T(2,128)} %edges_ref.1), custom_call_target="tpu_custom_call" | custom-call | tf_op jit(solution)/shard_map/densify/pallas_call | solution.py:60
  7.4 58.8 %train_step.1 = (f32[128,256]{1,0:T(8,128)}, f32[256,128]{1,0:T(8,128)}, f32[1,128]{1,0:T(1,128)}) custom-call(bf16[1024,512]{1,0:T(8,128)(2,1)} %densify.1.adj, bf16[128,128]{1,0:T(8,128)(2,1)} %feat.1, f32[1,128]{1,0:T(1,128)} %bitcast.4, bf16[128,256]{1,0:T(8,128)(2,1)} %w_in.1, bf16[256,128]{1,0:T(8,128)(2,1)} %w_out.1, s32[1,128]{1,0:T(1,128)} %bitcast.5), custom_call_target="tpu_custom_call" | custom-call | tf_op jit(solution)/shard_map/train_step/pallas_call | solution.py:280
  66.2 0.0 copy-start
  66.2 1.6 %copy.15 = f32[128,256]{1,0:T(8,128)} copy(f32[128,256]{1,0:T(8,128)} %get-tuple-element.12) | data formatting | bytes 262144
  67.8 0.0 copy-done
  67.8 0.0 copy-start.1
  67.8 0.7 copy.16
  68.4 0.0 copy-done.1
Async XLA Ops:
  66.2 1.6 %copy-start = (f32[256,128]{1,0:T(8,128)S(1)}, f32[256,128]{1,0:T(8,128)}, u32[]{:S(2)}) copy-start(f32[256,128]{1,0:T(8,128)} %get-tuple-element.13) | copy-start | bytes 393220
  67.8 0.7 copy-start.1

commit v4 on v3

--- a/solution.py
+++ b/solution.py
@@ -77,12 +77,11 @@
     grad_in, grad_out, loss_out,
     gath_one, part_one, recv_one, part_low, recv_low, gath_two, part_two, recv_two,
     gath_back, part_back, recv_back, part_grad, recv_grad, slots_grad, full_grad,
-    send_sem, recv_sem,
+    send_sem, recv_sem, *direct_refs,
 ):
     i = lax.axis_index("row")
     j = lax.axis_index("col")
     total_nodes = nd * R * C
-    chunk = full_grad.shape[0] // C
     pending = []
 
     def row_peer(k):
@@ -106,16 +105,18 @@
             copy.wait_recv()
 
     barrier = pltpu.get_barrier_semaphore()
-    for k in range(1, R):
-        pl.semaphore_signal(barrier, inc=1, device_id=row_peer(k), device_id_type=MESH)
-    for k in range(1, C):
-        pl.semaphore_signal(barrier, inc=1, device_id=col_peer(k), device_id_type=MESH)
+    greeted = [row_peer(k) for k in range(1, R)] + [col_peer(k) for k in range(1, C)]
+    others = [(a, b) for a in range(R) for b in range(C) if a + b > 0]
+    if direct_refs:
+        greeted = [(lax.rem(i + a, R), lax.rem(j + b, C)) for a, b in others]
+    for peer in greeted:
+        pl.semaphore_signal(barrier, inc=1, device_id=peer, device_id_type=MESH)
 
     scale = jnp.transpose(jnp.broadcast_to(norm[...], (nd, nd)))
     normed = (scale * feat[...].astype(F32)).astype(BF16)
     mine = pl.ds(pl.multiple_of(i * nd, nd), nd)
     gath_one[mine, :] = normed
-    pl.semaphore_wait(barrier, R + C - 2)
+    pl.semaphore_wait(barrier, len(greeted))
 
     def block_of(t):
         return adj[pl.ds(pl.multiple_of(t * nd, nd), nd), :]
@@ -176,7 +177,7 @@
         rows = rows.astype(F32)
         return rows[0:1, :] + rows[LOSS_ROWS // 2 : LOSS_ROWS // 2 + 1, :]
 
-    gath_back[j, :nd, :] = back_two
+    gath_back[j, :nd, :] = jnp.transpose(back_two.astype(F32)).astype(BF16)
     gath_back[j, nd:, :] = loss_rows(loss_local)
     copies = [send(4, k, col_peer(k), gath_back.at[j], gath_back.at[j]) for k in range(1, C)]
     arrive(low_copies)
@@ -192,9 +193,7 @@
     loss_col = read_loss(gath_back[0, nd:, :])
     for k in range(1, C):
         loss_col = loss_col + read_loss(gath_back[k, nd:, :])
-    values_t = jnp.transpose(
-        jnp.concatenate([gath_back[k, :nd, :] for k in range(C)], axis=0).astype(F32)
-    ).astype(BF16)
+    values_t = jnp.concatenate([gath_back[k, :nd, :] for k in range(C)], axis=1)
     rows_loss = loss_rows(loss_col)
 
     def back_of(t):
@@ -233,29 +232,59 @@
     base = fan_in * (hid // half)
     part_grad[base:, :] = local_out.astype(BF16)
 
+    chunk = full_grad.shape[0] // (R * C if direct_refs else C)
+
     def rows_of(t):
         return pl.ds(pl.multiple_of(t * chunk, chunk), chunk)
 
-    copies = [
-        send(6, k, col_peer(k), part_grad.at[rows_of(lax.rem(j + k, C))], recv_grad.at[k - 1])
-        for k in range(1, C)
-    ]
-    total = part_grad[rows_of(j), :].astype(F32)
-    for k in range(1, C):
-        copies[k - 1].wait_recv()
-        total = total + recv_grad[k - 1].astype(F32)
-    slots_grad[i] = total.astype(BF16)
-    arrive([send(7, k, row_peer(k), slots_grad.at[i], slots_grad.at[i]) for k in range(1, R)])
-    total = slots_grad[0].astype(F32)
-    for k in range(1, R):
-        total = total + slots_grad[k].astype(F32)
-    full_grad[rows_of(j), :] = total.astype(BF16)
-    arrive(
-        [
-            send(8, k, col_peer(k), full_grad.at[rows_of(j)], full_grad.at[rows_of(j)])
+    if direct_refs:
+        recv_all, send_all, sem_all = direct_refs
+
+        def send_to(phase, q, src, dst):
+            a, b = others[q]
+            copy = pltpu.make_async_remote_copy(
+                src_ref=src, dst_ref=dst,
+                send_sem=send_all.at[phase, q], recv_sem=sem_all.at[phase, q],
+                device_id=(lax.rem(i + a, R), lax.rem(j + b, C)), device_id_type=MESH,
+            )
+            copy.start()
+            pending.append(copy)
+            return copy
+
+        copies = []
+        for q, (a, b) in enumerate(others):
+            owner = lax.rem(i + a, R) * C + lax.rem(j + b, C)
+            copies.append(send_to(0, q, part_grad.at[rows_of(owner)], recv_all.at[q]))
+        own = rows_of(i * C + j)
+        total = part_grad[own, :].astype(F32)
+        for q in range(len(others)):
+            copies[q].wait_recv()
+            total = total + recv_all[q].astype(F32)
+        full_grad[own, :] = total.astype(BF16)
+        arrive(
+            [send_to(1, q, full_grad.at[own], full_grad.at[own]) for q in range(len(others))]
+        )
+    else:
+        copies = [
+            send(6, k, col_peer(k), part_grad.at[rows_of(lax.rem(j + k, C))], recv_grad.at[k - 1])
             for k in range(1, C)
         ]
-    )
+        total = part_grad[rows_of(j), :].astype(F32)
+        for k in range(1, C):
+            copies[k - 1].wait_recv()
+            total = total + recv_grad[k - 1].astype(F32)
+        slots_grad[i] = total.astype(BF16)
+        arrive([send(7, k, row_peer(k), slots_grad.at[i], slots_grad.at[i]) for k in range(1, R)])
+        total = slots_grad[0].astype(F32)
+        for k in range(1, R):
+            total = total + slots_grad[k].astype(F32)
+        full_grad[rows_of(j), :] = total.astype(BF16)
+        arrive(
+            [
+                send(8, k, col_peer(k), full_grad.at[rows_of(j)], full_grad.at[rows_of(j)])
+                for k in range(1, C)
+            ]
+        )
     for h in range(hid // half):
         grad_in[:, h * half : (h + 1) * half] = full_grad[h * fan_in : (h + 1) * fan_in, :].astype(
             F32
@@ -276,6 +305,13 @@
     grad_rows = (fan_in * hid + hid * classes) // TILE
     chunk = grad_rows // C
     most = max(R, C) - 1
+    direct = []
+    if grad_rows % (R * C * 16) == 0:
+        direct = [
+            pltpu.VMEM((R * C - 1, grad_rows // (R * C), TILE), BF16),
+            pltpu.SemaphoreType.DMA((2, R * C - 1)),
+            pltpu.SemaphoreType.DMA((2, R * C - 1)),
+        ]
     vmem = pl.BlockSpec(memory_space=pltpu.VMEM)
     grad_in, grad_out, loss = pl.pallas_call(
         functools.partial(step_kernel, R, C, nd),
@@ -304,6 +340,7 @@
             pltpu.VMEM((grad_rows, TILE), BF16),
             pltpu.SemaphoreType.DMA((10, most)),
             pltpu.SemaphoreType.DMA((10, most)),
+            *direct,
         ],
         compiler_params=pltpu.CompilerParams(
             collective_id=0, has_side_effects=True, vmem_limit_bytes=VMEM_LIMIT

time: 70 us -> 69.7 us (level)
  no operation moved by 1% of the time
where the time goes in v4:
time: 69.7 us; the launch traced here: 69.6 us
  Pallas kernels  64.9 us (93%)
  between operations  2.46 us (4%)
  local copies, waits for them, and re-layouts  2.27 us (3%)
    pallas_call x1, Pallas kernels, per_device(): pl.pallas_call(functools.partial(step_kernel, R, C, nd), out_shape=(jax.S...  58.7 us
    pallas_call x1, Pallas kernels, densify(): pl.pallas_call(functools.partial(densify_kernel, row_tiles, col_tiles), o...  6.12 us
    unnamed x6, local copies, waits for them, and re-layouts  2.27 us

profile of v4, /device:TPU:0, one launch (start us, length us, event | category | flops | bytes accessed | tf_op | source)
XLA Modules:
  0.0 69.6 jit_solution(18269331403911737988)
XLA Ops:
  1.3 6.1 %densify.1.adj = bf16[1024,512]{1,0:T(8,128)(2,1)} custom-call(s32[1]{0:T(128)S(6)} %copy.14.count_ref, s32[1,128]{1,0:T(1,128)} %slot_ref.1, s32[1,128,2,512]{3,2,1,0:T(2,128)} %edges_ref.1), custom_call_target="tpu_custom_call" | custom-call | tf_op jit(solution)/shard_map/densify/pallas_call | solution.py:60
  7.4 58.7 %train_step.1 = (f32[128,256]{1,0:T(8,128)}, f32[256,128]{1,0:T(8,128)}, f32[1,128]{1,0:T(1,128)}) custom-call(bf16[1024,512]{1,0:T(8,128)(2,1)} %densify.1.adj, bf16[128,128]{1,0:T(8,128)(2,1)} %feat.1, f32[1,128]{1,0:T(1,128)} %bitcast.4, bf16[128,256]{1,0:T(8,128)(2,1)} %w_in.1, bf16[256,128]{1,0:T(8,128)(2,1)} %w_out.1, s32[1,128]{1,0:T(1,128)} %bitcast.5), custom_call_target="tpu_custom_call" | custom-call | tf_op jit(solution)/shard_map/train_step/pallas_call | solution.py:316
  66.1 0.0 copy-start
  66.2 1.6 %copy.15 = f32[128,256]{1,0:T(8,128)} copy(f32[128,256]{1,0:T(8,128)} %get-tuple-element.12) | data formatting | bytes 262144
  67.8 0.0 copy-done
  67.8 0.0 copy-start.1
  67.8 0.7 copy.16
  68.4 0.0 copy-done.1
Async XLA Ops:
  66.1 1.6 %copy-start = (f32[256,128]{1,0:T(8,128)S(1)}, f32[256,128]{1,0:T(8,128)}, u32[]{:S(2)}) copy-start(f32[256,128]{1,0:T(8,128)} %get-tuple-element.13) | copy-start | bytes 393220
  67.8 0.7 copy-start.1
